TPU v7x, 256 devices: a whole 4x4x8 slice. The times are simulated.
256 devices in a mesh: rows: 32 (over y, x, core), cols: 8 (over z).
Axes of the slice: x: 4, y: 4, z: 8, core: 2. Of those that a mesh axis runs over, the one named last changes fastest.
Arguments:
- latent: float32 [2048, 16384], P('rows', 'cols'), may hold values from -3 to 3
- counts: int32 [2048, 16384], P('rows', 'cols'), may hold values from 0 to 39
- exposure: int32 [2048, 16384], P('rows', 'cols'), may hold values from 1 to 32
Outputs:
- newton_step: float32 [2048, 16384], P('rows', 'cols')
- residual: float32 [2048, 16384], P('rows', 'cols')
- direction: float32 [2048, 16384], P('rows', 'cols')
All inputs are finite; a program needn't handle non-finite values.
Results may differ from a plain program's by a relative error of at most 0.0003.
Values sent between devices are 32-bit elements; how exact they have to be, the bound alone decides.
No kernel may reach another device: no remote copies, remote signals or barrier semaphores. Data moves between devices by JAX's collectives and lax.ppermute only.
A program may use at most 128 MiB of HBM per device.

v0:
```python
import math
import jax
import jax.numpy as jnp
from jax import lax
from jax.sharding import PartitionSpec as P

dispersion = 4.0
prior_scale = 0.25
kappa_sq = 0.05
weight_shift = 1.0
highest = lax.Precision.HIGHEST


def extended(cells, sides, width):
    for axis, dim in sides:
        count = lax.axis_size(axis)
        ends = count - 1
        head = lax.slice_in_dim(cells, 0, width, axis=dim)
        tail = lax.slice_in_dim(cells, cells.shape[dim] - width, cells.shape[dim], axis=dim)
        cells = jnp.concatenate(
            [
                lax.ppermute(tail, axis, [(i, (i + 1) % count) for i in range(ends)]),
                cells,
                lax.ppermute(head, axis, [((i + 1) % count, i) for i in range(ends)]),
            ],
            axis=dim,
        )
    return cells


def dft_table(length):
    index_line = lax.iota(jnp.int32, length)
    product = index_line[:, None] * index_line[None, :] % length
    angle = 2.0 * math.pi / length * product.astype(jnp.float32)
    return (jnp.cos(angle), jnp.sin(angle))


def twiddle_table(outer_len, inner_len):
    product = lax.iota(jnp.int32, outer_len)[:, None] * lax.iota(jnp.int32, inner_len)[None, :]
    angle = 2.0 * math.pi / (outer_len * inner_len) * product.astype(jnp.float32)
    return (jnp.cos(angle), jnp.sin(angle))


def left_apply(table, data):
    return jnp.dot(table, data, precision=highest)


def middle_apply(table, data):
    return jnp.einsum("ka,lab->lkb", table, data, precision=highest)


def last_apply(data, table):
    line_rows, outer_len, inner_len = data.shape
    flat = jnp.dot(data.reshape(line_rows * outer_len, inner_len), table, precision=highest)
    return flat.reshape(line_rows, outer_len, inner_len)


def split_lengths(total_cols):
    inner_len = math.gcd(total_cols, 128)
    return (total_cols // inner_len, inner_len)


def columns_forward(real_part, imag_part):
    line_rows, total_cols = real_part.shape
    outer_len, inner_len = split_lengths(total_cols)
    outer_cos, outer_sin = dft_table(outer_len)
    inner_cos, inner_sin = dft_table(inner_len)
    twist_cos, twist_sin = twiddle_table(outer_len, inner_len)
    real_cube = real_part.reshape(line_rows, outer_len, inner_len)
    imag_cube = imag_part.reshape(line_rows, outer_len, inner_len)
    section_real = middle_apply(outer_cos, real_cube) + middle_apply(outer_sin, imag_cube)
    section_imag = middle_apply(outer_cos, imag_cube) - middle_apply(outer_sin, real_cube)
    turned_real = section_real * twist_cos + section_imag * twist_sin
    turned_imag = section_imag * twist_cos - section_real * twist_sin
    final_real = last_apply(turned_real, inner_cos) + last_apply(turned_imag, inner_sin)
    final_imag = last_apply(turned_imag, inner_cos) - last_apply(turned_real, inner_sin)
    return (final_real.reshape(line_rows, total_cols), final_imag.reshape(line_rows, total_cols))


def columns_inverse(real_part, imag_part):
    line_rows, total_cols = real_part.shape
    outer_len, inner_len = split_lengths(total_cols)
    outer_cos, outer_sin = dft_table(outer_len)
    inner_cos, inner_sin = dft_table(inner_len)
    twist_cos, twist_sin = twiddle_table(outer_len, inner_len)
    real_cube = real_part.reshape(line_rows, outer_len, inner_len)
    imag_cube = imag_part.reshape(line_rows, outer_len, inner_len)
    section_real = last_apply(real_cube, inner_cos) - last_apply(imag_cube, inner_sin)
    section_imag = last_apply(imag_cube, inner_cos) + last_apply(real_cube, inner_sin)
    turned_real = section_real * twist_cos - section_imag * twist_sin
    turned_imag = section_imag * twist_cos + section_real * twist_sin
    final_real = middle_apply(outer_cos, turned_real) - middle_apply(outer_sin, turned_imag)
    final_imag = middle_apply(outer_cos, turned_imag) + middle_apply(outer_sin, turned_real)
    return (final_real.reshape(line_rows, total_cols), final_imag.reshape(line_rows, total_cols))


def inverse_symbol(row_freq, col_freq, band_rows, total_cols):
    row_sine = jnp.sin(math.pi * row_freq.astype(jnp.float32) / band_rows)
    col_sine = jnp.sin(math.pi * col_freq.astype(jnp.float32) / total_cols)
    inner_term = kappa_sq + 4.0 * row_sine * row_sine + 4.0 * col_sine * col_sine
    symbol = prior_scale * inner_term * inner_term + weight_shift
    quarter = total_cols // 4
    retained = (col_freq < quarter) | (col_freq > total_cols - quarter)
    weight = jnp.where(retained, 1.0 / symbol, 1.0)
    return weight / float(band_rows * total_cols)


def frequency_of(position, outer_len, inner_len):
    return position // inner_len + outer_len * (position % inner_len)


def precondition(grid_field):
    band_rows, block_cols = grid_field.shape
    col_parts = lax.axis_size("cols")
    col_index = lax.axis_index("cols")
    total_cols = block_cols * col_parts
    outer_len, inner_len = split_lengths(total_cols)
    row_cos, row_sin = dft_table(band_rows)
    spectrum = jnp.stack([left_apply(row_cos, grid_field), -left_apply(row_sin, grid_field)])
    whole_lines = lax.all_to_all(spectrum, "cols", split_axis=1, concat_axis=2, tiled=True)
    line_rows = band_rows // col_parts
    spec_real, spec_imag = columns_forward(whole_lines[0], whole_lines[1])
    row_freq = col_index * line_rows + lax.iota(jnp.int32, line_rows)
    col_freq = frequency_of(lax.iota(jnp.int32, total_cols), outer_len, inner_len)
    spectral_scale = inverse_symbol(row_freq[:, None], col_freq[None, :], band_rows, total_cols)
    back_real, back_imag = columns_inverse(spec_real * spectral_scale, spec_imag * spectral_scale)
    blocks = lax.all_to_all(
        jnp.stack([back_real, back_imag]), "cols", split_axis=2, concat_axis=1, tiled=True
    )
    return left_apply(row_cos, blocks[0]) - left_apply(row_sin, blocks[1])


def prior_apply(grid_field):
    padded = extended(grid_field, (("rows", 0), ("cols", 1)), 2)
    row_count, col_count = grid_field.shape

    def offset_view(shift_row, shift_col):
        return padded[
            2 + shift_row : 2 + shift_row + row_count, 2 + shift_col : 2 + shift_col + col_count
        ]

    centre = kappa_sq + 4.0
    nearest = offset_view(1, 0) + offset_view(-1, 0) + offset_view(0, 1) + offset_view(0, -1)
    diagonal = offset_view(1, 1) + offset_view(1, -1) + offset_view(-1, 1) + offset_view(-1, -1)
    distant = offset_view(2, 0) + offset_view(-2, 0) + offset_view(0, 2) + offset_view(0, -2)
    return prior_scale * (
        (centre * centre + 4.0) * grid_field - 2.0 * centre * nearest + 2.0 * diagonal + distant
    )


def on_device(latent, counts, exposure):
    mean_rate = exposure.astype(jnp.float32) * jnp.exp(latent)
    fisher = dispersion * mean_rate / (dispersion + mean_rate)
    score = (counts.astype(jnp.float32) - mean_rate) * dispersion / (dispersion + mean_rate)
    gradient = score - prior_apply(latent)
    first_search = precondition(gradient)
    first_product = lax.psum(jnp.sum(gradient * first_search), ("rows", "cols"))
    image = prior_apply(first_search) + fisher * first_search
    curvature = lax.psum(jnp.sum(first_search * image), ("rows", "cols"))
    step_size = first_product / curvature
    residual = gradient - step_size * image
    next_search = precondition(residual)
    next_product = lax.psum(jnp.sum(residual * next_search), ("rows", "cols"))
    newton_step = step_size * first_search
    direction = next_search + next_product / first_product * first_search
    return (newton_step, residual, direction)


def solution(mesh):
    placed = (P("rows", "cols"), P("rows", "cols"), P("rows", "cols"))
    return jax.shard_map(
        on_device,
        mesh=mesh,
        in_specs=placed,
        out_specs=(P("rows", "cols"), P("rows", "cols"), P("rows", "cols")),
        check_vma=False,
    )
```

profile of v0, /device:TPU:1, one launch (start us, length us, event | category | flops | bytes accessed | tf_op | source)
XLA Modules:
  0.0 564.2 jit_solution(15677637600210697787)
XLA Ops:
  1.5 5.1 collective-permute-start
  11.9 4.0 collective-permute-start.3
  18.4 2.9 fusion.34
  24.6 9.9 %all-to-all-start = ((f32[2,64,2048]{2,0,1:T(2,128)}), f32[2,64,2048]{2,0,1:T(2,128)S(1)}, u32[]{:S(2)}, u32[]{:S(2)}) async-start(f32[2,64,2048]{2,0,1:T(2,128)} %copy.128), calls=%async_computation | async-start | bytes 2097152 | tf_op jit(solution)/shard_map/all_to_all | solution.py:120
  35.6 27.9 %all-to-all-done = f32[2,64,2048]{2,0,1:T(2,128)S(1)} async-done(((f32[2,64,2048]{2,0,1:T(2,128)}), f32[2,64,2048]{2,0,1:T(2,128)S(1)}, u32[]{:S(2)}, u32[]{:S(2)}) %all-to-all-start) | async-done | bytes 1048608 | tf_op jit(solution)/shard_map/all_to_all | solution.py:120
  83.7 14.7 %copy.146 = f32[2,8,16384]{1,0,2:T(2,128)} copy(f32[2,8,16384]{2,1,0:T(8,128)S(1)} %pad_maximum_fusion.1) | data formatting | bytes 2097152 | tf_op jit(solution)/shard_map/stack | solution.py:128
  98.4 28.3 %reshape.237 = f32[8,1,32768]{2,1,0:T(1,128)S(1)} reshape(f32[16384,2,8]{2,1,0:T(2,128)} %bitcast.148) | data formatting | bytes 2097152
  126.7 31.4 %all_to_all.60 = f32[8,1,32768]{2,1,0:T(1,128)S(1)} all-to-all(f32[8,1,32768]{2,1,0:T(1,128)S(1)} %reshape.237), channel_id=1, replica_groups=mesh['rows'=32,'cols'=8] {'cols'}, dimensions={0} | all-to-all | bytes 2097152 | tf_op jit(solution)/shard_map/all_to_all | solution.py:127
  158.7 3.2 reduce
  161.9 32.3 %reshape.238 = f32[16384,2,8]{2,1,0:T(2,128)} reshape(f32[8,32768]{1,0:T(8,128)S(1)} %reduce) | data formatting | bytes 2097152
  194.2 13.2 %copy.194 = f32[2,8,8,2048]{3,2,1,0:T(8,128)S(1)} copy(f32[2,8,8,2048]{1,0,3,2:T(2,128)} %bitcast.149) | data formatting | bytes 2097152 | tf_op jit(solution)/shard_map/all_to_all | solution.py:127
  211.3 2.4 collective-permute-start.4
  213.8 2.6 collective-permute-done.4
  217.8 4.0 collective-permute-start.7
  224.9 79.0 %all-reduce = (f32[]{:T(128)}, f32[]{:T(128)}) all-reduce(f32[]{:T(128)} %get-tuple-element.4, f32[]{:T(128)} %get-tuple-element.3), channel_id=1, replica_groups=mesh['rows'=32,'cols'=8] {'rows','cols'}, use_global_device_ids=true, to_apply=%region_1.2 | all-reduce | flops 2 | bytes 16 | tf_op jit(solution)/shard_map/psum | solution.py:157
  307.6 31.7 %all_to_all.61 = f32[2,64,2048]{2,0,1:T(2,128)S(1)} all-to-all(f32[2,64,2048]{2,0,1:T(2,128)S(1)} %copy.150), channel_id=1, replica_groups=mesh['rows'=32,'cols'=8] {'cols'}, dimensions={1} | all-to-all | bytes 2097152 | tf_op jit(solution)/shard_map/all_to_all | solution.py:120
  356.9 1.9 stack_reshape.15
  361.1 14.7 %copy.166 = f32[2,8,16384]{1,0,2:T(2,128)} copy(f32[2,8,16384]{2,1,0:T(8,128)S(1)} %pad_maximum_fusion.3) | data formatting | bytes 2097152 | tf_op jit(solution)/shard_map/stack | solution.py:128
  375.8 28.3 %reshape.239 = f32[8,1,32768]{2,1,0:T(1,128)S(1)} reshape(f32[16384,2,8]{2,1,0:T(2,128)} %bitcast.150) | data formatting | bytes 2097152
  404.1 28.8 %all_to_all.62 = f32[8,1,32768]{2,1,0:T(1,128)} all-to-all(f32[8,1,32768]{2,1,0:T(1,128)S(1)} %reshape.239), channel_id=1, replica_groups=mesh['rows'=32,'cols'=8] {'cols'}, dimensions={0} | all-to-all | bytes 2097152 | tf_op jit(solution)/shard_map/all_to_all | solution.py:127
  432.9 4.4 reduce.1
  437.3 32.1 %reshape.240 = f32[16384,2,8]{2,1,0:T(2,128)} reshape(f32[8,32768]{1,0:T(8,128)S(1)} %reduce.1) | data formatting | bytes 2097152
  469.4 13.2 %copy.195 = f32[2,8,8,2048]{3,2,1,0:T(8,128)S(1)} copy(f32[2,8,8,2048]{1,0,3,2:T(2,128)} %bitcast.151) | data formatting | bytes 2097152 | tf_op jit(solution)/shard_map/all_to_all | solution.py:127
  485.2 76.5 %psum.23 = f32[]{:T(128)} all-reduce(f32[]{:T(128)} %get-tuple-element.30), channel_id=1, replica_groups=mesh['rows'=32,'cols'=8] {'rows','cols'}, use_global_device_ids=true, to_apply=%region_5.6 | all-reduce | flops 1 | bytes 8 | tf_op jit(solution)/shard_map/psum | solution.py:163
  (99 shorter events, 67.7 us)
Async XLA Ops:
  1.5 8.2 %collective-permute-start = (f32[2,2048]{1,0:T(2,128)S(1)}, f32[2,2048]{1,0:T(2,128)S(1)}, u32[]{:S(2)}, u32[]{:S(2)}) collective-permute-start(f32[2,2048]{1,0:T(2,128)S(1)} %get-tuple-element.28), channel_id=1, source_target_pairs={{8,0},{16,8},{24,16},{32,24},{40,32},{48,40},{56,48},{64,56},{72,6... | collective-permute-start | bytes 49160 | tf_op jit(solution)/shard_map/ppermute | solution.py:24
  6.7 3.1 collective-permute-start.1
  10.6 5.3 collective-permute-start.2
  11.9 5.0 collective-permute-start.3
  24.6 38.8 %all-to-all-start = ((f32[2,64,2048]{2,0,1:T(2,128)}), f32[2,64,2048]{2,0,1:T(2,128)S(1)}, u32[]{:S(2)}, u32[]{:S(2)}) async-start(f32[2,64,2048]{2,0,1:T(2,128)} %copy.128), calls=%async_computation | async-start | bytes 2097152 | tf_op jit(solution)/shard_map/all_to_all | solution.py:120
  194.2 28.9 %copy-start = (f32[64,2048]{1,0:T(8,128)S(1)}, f32[64,2048]{1,0:T(8,128)}, u32[]{:S(2)}) copy-start(f32[64,2048]{1,0:T(8,128)} %param.3) | copy-start | bytes 1572868
  194.2 28.9 %copy-start.2 = (s32[64,2048]{1,0:T(8,128)S(1)}, s32[64,2048]{1,0:T(8,128)}, u32[]{:S(2)}) copy-start(s32[64,2048]{1,0:T(8,128)} %param.5) | copy-start | bytes 1572868
  209.4 4.3 collective-permute-start.5
  211.3 5.1 collective-permute-start.4
  216.5 5.3 collective-permute-start.6
  217.8 5.0 collective-permute-start.7
  305.3 178.3 %copy-start.1 = (f32[64,2048]{1,0:T(8,128)}, f32[64,2048]{1,0:T(8,128)S(1)}, u32[]{:S(2)}) copy-start(f32[64,2048]{1,0:T(8,128)S(1)} %multiply_subtract_fusion.2) | copy-start | bytes 1572868
where the time goes:
time: 569 us; the launch traced here: 564 us
  blocking collectives  247 us (43%)
  local copies, waits for them, and re-layouts  189 us (33%)
  matrix products  40.4 us (7%)
  waiting for transfers between devices  32.6 us (6%)
  starting transfers between devices  31.8 us (6%)
  other arithmetic  19.3 us (3%)
    unnamed x11, local copies, waits for them, and re-layouts  122 us
    psum x1, blocking collectives, on_device(): first_product = lax.psum(jnp.sum(gradient * first_search), ('rows', 'cols'))  79 us
    psum x1, blocking collectives, on_device(): next_product = lax.psum(jnp.sum(residual * next_search), ('rows', 'cols'))  76.5 us
    all_to_all x2, blocking collectives, precondition(): lax.all_to_all(jnp.stack([back_real, back_imag]), 'cols', split_axis=2, c...  60.2 us
    another operation x6, local copies, waits for them, and re-layouts, precondition(): jnp.stack([back_real, back_imag])  32.4 us
    all_to_all x1, blocking collectives, precondition(): lax.all_to_all(spectrum, 'cols', split_axis=1, concat_axis=2, tiled=True)  31.7 us
    all_to_all x1, waiting for transfers between devices, precondition(): lax.all_to_all(spectrum, 'cols', split_axis=1, concat_axis=2, tiled=True)  27.9 us
    all_to_all x3, local copies, waits for them, and re-layouts, precondition(): lax.all_to_all(jnp.stack([back_real, back_imag]), 'cols', split_axis=2, c...  27 us
  transfers between devices with their start and end apart: 9, of which 5 were waited for; matrix products, arithmetic and copies ran while one was open for 0% of the time, Pallas kernels for 0%

commit v1 on v0

--- a/solution.py
+++ b/solution.py
@@ -9,6 +9,30 @@
 kappa_sq = 0.05
 weight_shift = 1.0
 highest = lax.Precision.HIGHEST
+
+
+def split_up(x, dim, count):
+    shape = x.shape
+    pieces = x.reshape(*shape[:dim], count, shape[dim] // count, *shape[dim + 1 :])
+    return jnp.moveaxis(pieces, dim, 0)
+
+
+def joined_along(pieces, dim):
+    lengths = list(pieces.shape[1:])
+    lengths[dim] *= pieces.shape[0]
+    return jnp.moveaxis(pieces, 0, dim).reshape(lengths)
+
+
+def sent_to_each(x, axis, split_dim, concat_dim):
+    length, index = (lax.axis_size(axis), lax.axis_index(axis))
+    tiles = split_up(x, split_dim, length)
+    whole = tiles
+    for step in range(1, length):
+        target, source = ((index + step) % length, (index - step) % length)
+        sent = lax.dynamic_index_in_dim(tiles, target, 0)
+        theirs = lax.ppermute(sent, axis, [(i, (i + step) % length) for i in range(length)])
+        whole = lax.dynamic_update_slice_in_dim(whole, theirs, source, axis=0)
+    return joined_along(whole, concat_dim)
 
 
 def extended(cells, sides, width):
@@ -124,9 +148,7 @@
     col_freq = frequency_of(lax.iota(jnp.int32, total_cols), outer_len, inner_len)
     spectral_scale = inverse_symbol(row_freq[:, None], col_freq[None, :], band_rows, total_cols)
     back_real, back_imag = columns_inverse(spec_real * spectral_scale, spec_imag * spectral_scale)
-    blocks = lax.all_to_all(
-        jnp.stack([back_real, back_imag]), "cols", split_axis=2, concat_axis=1, tiled=True
-    )
+    blocks = sent_to_each(jnp.stack([back_real, back_imag]), "cols", 2, 1)
     return left_apply(row_cos, blocks[0]) - left_apply(row_sin, blocks[1])
 
 

time: 569 us -> 390 us (0.69)
  local copies, waits for them, and re-layouts: 189 us -> 40 us
  blocking collectives: 247 us -> 187 us
  starting transfers between devices: 31.8 us -> 52 us
  waiting for transfers between devices: 32.6 us -> 52 us
  other arithmetic: 19.3 us -> 5.89 us
    unnamed x11 -> x29, local copies, waits for them, and re-layouts: 122 us -> 4.49 us
    all_to_all x2 -> x0, blocking collectives: 60.2 us -> none  [precondition(): lax.all_to_all(jnp.stack([back_real, back_imag]), 'cols', split_axis=2, c...]
    another operation x6, local copies, waits for them, and re-layouts: 32.4 us -> 4.07 us  [precondition(): blocks = sent_to_each(jnp.stack([back_real, back_imag]), 'cols', 2, 1)]
    all_to_all x3 -> x0, local copies, waits for them, and re-layouts: 27 us -> none  [precondition(): lax.all_to_all(jnp.stack([back_real, back_imag]), 'cols', split_axis=2, c...]
    ppermute x0 -> x14, starting transfers between devices: none -> 20 us  [sent_to_each(): lax.ppermute(sent, axis, [(i, (i + step) % length) for i in range(length)])]
    ppermute x0 -> x14, waiting for transfers between devices: none -> 19.6 us  [sent_to_each(): lax.ppermute(sent, axis, [(i, (i + step) % length) for i in range(length)])]
    dynamic_update_slice x0 -> x14, local copies, waits for them, and re-layouts: none -> 19.5 us  [sent_to_each(): whole = lax.dynamic_update_slice_in_dim(whole, theirs, source, axis=0)]
    all_to_all x2 -> x0, other arithmetic: 7.58 us -> none  [precondition(): lax.all_to_all(jnp.stack([back_real, back_imag]), 'cols', split_axis=2, c...]
  transfers between devices with their start and end apart: 9 -> 23, of which waited for: 5 -> 9; matrix products, arithmetic and copies ran while one was open for 0% -> 5% of each run, Pallas kernels for 0% -> 0%
where the time goes in v1:
time: 390 us; the launch traced here: 384 us
  blocking collectives  187 us (48%)
  starting transfers between devices  52 us (13%)
  waiting for transfers between devices  52 us (13%)
  matrix products  42.2 us (11%)
  local copies, waits for them, and re-layouts  40 us (10%)
  other arithmetic  5.89 us (2%)
  between operations  4.44 us (1%)
    psum x1, blocking collectives, on_device(): first_product = lax.psum(jnp.sum(gradient * first_search), ('rows', 'cols'))  79.6 us
    psum x1, blocking collectives, on_device(): next_product = lax.psum(jnp.sum(residual * next_search), ('rows', 'cols'))  75.8 us
    all_to_all x1, blocking collectives, precondition(): lax.all_to_all(spectrum, 'cols', split_axis=1, concat_axis=2, tiled=True)  32 us
    all_to_all x1, waiting for transfers between devices, precondition(): lax.all_to_all(spectrum, 'cols', split_axis=1, concat_axis=2, tiled=True)  27.7 us
    ppermute x14, starting transfers between devices, sent_to_each(): lax.ppermute(sent, axis, [(i, (i + step) % length) for i in range(length)])  20 us
    ppermute x14, waiting for transfers between devices, sent_to_each(): lax.ppermute(sent, axis, [(i, (i + step) % length) for i in range(length)])  19.6 us
    dynamic_update_slice x14, local copies, waits for them, and re-layouts, sent_to_each(): whole = lax.dynamic_update_slice_in_dim(whole, theirs, source, axis=0)  19.5 us
    dot_general x16, matrix products, last_apply(): jnp.dot(data.reshape(line_rows * outer_len, inner_len), table, precision=...  17.8 us
  transfers between devices with their start and end apart: 23, of which 9 were waited for; matrix products, arithmetic and copies ran while one was open for 5% of the time, Pallas kernels for 0%

profile of v1, /device:TPU:1, one launch (start us, length us, event | category | flops | bytes accessed | tf_op | source)
XLA Modules:
  0.0 384.1 jit_solution(5879156798381828356)
XLA Ops:
  1.5 5.1 %collective-permute-start = (f32[2,2048]{1,0:T(2,128)S(1)}, f32[2,2048]{1,0:T(2,128)S(1)}, u32[]{:S(2)}, u32[]{:S(2)}) collective-permute-start(f32[2,2048]{1,0:T(2,128)S(1)} %get-tuple-element.42), channel_id=1, source_target_pairs={{8,0},{16,8},{24,16},{32,24},{40,32},{48,40},{56,48},{64,56},{72,6... | collective-permute-start | bytes 49160 | tf_op jit(solution)/shard_map/ppermute | solution.py:48
  6.7 2.1 collective-permute-start.1
  11.3 4.0 %collective-permute-start.3 = (f32[68,2]{1,0:T(8,128)S(1)}, f32[68,2]{1,0:T(8,128)S(1)}, u32[]{:S(2)}, u32[]{:S(2)}) collective-permute-start(f32[68,2]{1,0:T(8,128)S(1)} %get-tuple-element.37), channel_id=1, source_target_pairs={{0,1},{1,2},{2,3},{3,4},{4,5},{5,6},{6,7},{8,9},{9,10},{10,11},{11... | collective-permute-start | bytes 1640 | tf_op jit(solution)/shard_map/ppermute | solution.py:46
  21.1 9.9 %all-to-all-start = ((f32[2,64,2048]{2,0,1:T(2,128)}), f32[2,64,2048]{2,0,1:T(2,128)S(1)}, u32[]{:S(2)}, u32[]{:S(2)}) async-start(f32[2,64,2048]{2,0,1:T(2,128)} %copy.60), calls=%async_computation | async-start | bytes 2097152 | tf_op jit(solution)/shard_map/all_to_all | solution.py:144
  32.3 27.7 %all-to-all-done = f32[2,64,2048]{2,0,1:T(2,128)S(1)} async-done(((f32[2,64,2048]{2,0,1:T(2,128)}), f32[2,64,2048]{2,0,1:T(2,128)S(1)}, u32[]{:S(2)}, u32[]{:S(2)}) %all-to-all-start) | async-done | bytes 1048608 | tf_op jit(solution)/shard_map/all_to_all | solution.py:144
  77.7 2.0 copy.77
  86.8 4.7 %collective-permute-start.8 = (f32[1,2,8,2048]{3,0,2,1:T(1,128)S(1)}, f32[1,2,8,2048]{3,0,2,1:T(1,128)S(1)}, u32[]{:S(2)}, u32[]{:S(2)}) collective-permute-start(f32[1,2,8,2048]{3,0,2,1:T(1,128)S(1)} %get-tuple-element.23), channel_id=1, source_target_pairs={{0,5},{1,6},{2,7},{3,0},{4,1},{5,2},{6,3},{7,4},{8,13},{9,14},{10,... | collective-permute-start | bytes 393224 | tf_op jit(solution)/shard_map/ppermute | solution.py:33
  93.5 2.7 collective-permute-start.9
  97.2 2.0 dynamic_update_slice.42
  99.2 2.1 dynamic_update_slice.43
  101.3 2.1 dynamic_update_slice.44
  103.4 8.7 %collective-permute-done.7 = f32[1,2,8,2048]{3,0,2,1:T(1,128)} collective-permute-done((f32[1,2,8,2048]{3,0,2,1:T(1,128)S(1)}, f32[1,2,8,2048]{3,0,2,1:T(1,128)}, u32[]{:S(2)}, u32[]{:S(2)}) %collective-permute-start.7) | collective-permute-done | bytes 131104 | tf_op jit(solution)/shard_map/ppermute | solution.py:33
  112.1 2.0 dynamic_update_slice.45
  114.9 2.1 dynamic_update_slice.47
  117.0 2.1 dynamic_update_slice.48
  122.9 2.4 collective-permute-start.11
  125.4 2.6 collective-permute-done.11
  129.4 4.1 %collective-permute-start.14 = (f32[68,2]{1,0:T(8,128)S(1)}, f32[68,2]{1,0:T(8,128)S(1)}, u32[]{:S(2)}, u32[]{:S(2)}) collective-permute-start(f32[68,2]{1,0:T(8,128)S(1)} %get-tuple-element.33), channel_id=1, source_target_pairs={{0,1},{1,2},{2,3},{3,4},{4,5},{5,6},{6,7},{8,9},{9,10},{10,11},{11... | collective-permute-start | bytes 1640 | tf_op jit(solution)/shard_map/ppermute | solution.py:46
  136.6 79.6 %all-reduce = (f32[]{:T(128)}, f32[]{:T(128)}) all-reduce(f32[]{:T(128)} %get-tuple-element.4, f32[]{:T(128)} %get-tuple-element.3), channel_id=1, replica_groups=mesh['rows'=32,'cols'=8] {'rows','cols'}, use_global_device_ids=true, to_apply=%region_1.2 | all-reduce | flops 2 | bytes 16 | tf_op jit(solution)/shard_map/psum | solution.py:179
  220.0 32.0 %all_to_all.30 = f32[2,64,2048]{2,0,1:T(2,128)S(1)} all-to-all(f32[2,64,2048]{2,0,1:T(2,128)S(1)} %copy.80), channel_id=1, replica_groups=mesh['rows'=32,'cols'=8] {'cols'}, dimensions={1} | all-to-all | bytes 2097152 | tf_op jit(solution)/shard_map/all_to_all | solution.py:144
  275.9 3.8 collective-permute-start.19
  281.8 2.8 collective-permute-start.20
  290.2 9.3 %collective-permute-done.18 = f32[1,2,8,2048]{3,0,2,1:T(1,128)S(1)} collective-permute-done((f32[1,2,8,2048]{3,0,2,1:T(1,128)S(1)}, f32[1,2,8,2048]{3,0,2,1:T(1,128)S(1)}, u32[]{:S(2)}, u32[]{:S(2)}) %collective-permute-start.18) | collective-permute-done | bytes 131104 | tf_op jit(solution)/shard_map/ppermute | solution.py:33
  305.7 75.8 %psum.23 = f32[]{:T(128)} all-reduce(f32[]{:T(128)} %get-tuple-element.44), channel_id=1, replica_groups=mesh['rows'=32,'cols'=8] {'rows','cols'}, use_global_device_ids=true, to_apply=%region_5.6 | all-reduce | flops 1 | bytes 8 | tf_op jit(solution)/shard_map/psum | solution.py:185
  (152 shorter events, 88.0 us)
Async XLA Ops:
  1.5 8.3 %collective-permute-start = (f32[2,2048]{1,0:T(2,128)S(1)}, f32[2,2048]{1,0:T(2,128)S(1)}, u32[]{:S(2)}, u32[]{:S(2)}) collective-permute-start(f32[2,2048]{1,0:T(2,128)S(1)} %get-tuple-element.42), channel_id=1, source_target_pairs={{8,0},{16,8},{24,16},{32,24},{40,32},{48,40},{56,48},{64,56},{72,6... | collective-permute-start | bytes 49160 | tf_op jit(solution)/shard_map/ppermute | solution.py:48
  6.7 3.2 collective-permute-start.1
  10.0 5.3 %collective-permute-start.2 = (f32[68,2]{1,0:T(8,128)S(1)}, f32[68,2]{1,0:T(8,128)S(1)}, u32[]{:S(2)}, u32[]{:S(2)}) collective-permute-start(f32[68,2]{1,0:T(8,128)S(1)} %get-tuple-element.36), channel_id=1, source_target_pairs={{1,0},{2,1},{3,2},{4,3},{5,4},{6,5},{7,6},{9,8},{10,9},{11,10},{12... | collective-permute-start | bytes 1640 | tf_op jit(solution)/shard_map/ppermute | solution.py:48
  11.3 5.0 %collective-permute-start.3 = (f32[68,2]{1,0:T(8,128)S(1)}, f32[68,2]{1,0:T(8,128)S(1)}, u32[]{:S(2)}, u32[]{:S(2)}) collective-permute-start(f32[68,2]{1,0:T(8,128)S(1)} %get-tuple-element.37), channel_id=1, source_target_pairs={{0,1},{1,2},{2,3},{3,4},{4,5},{5,6},{6,7},{8,9},{9,10},{10,11},{11... | collective-permute-start | bytes 1640 | tf_op jit(solution)/shard_map/ppermute | solution.py:46
  21.1 38.9 %all-to-all-start = ((f32[2,64,2048]{2,0,1:T(2,128)}), f32[2,64,2048]{2,0,1:T(2,128)S(1)}, u32[]{:S(2)}, u32[]{:S(2)}) async-start(f32[2,64,2048]{2,0,1:T(2,128)} %copy.60), calls=%async_computation | async-start | bytes 2097152 | tf_op jit(solution)/shard_map/all_to_all | solution.py:144
  86.6 6.8 %collective-permute-start.5 = (f32[1,2,8,2048]{3,0,2,1:T(1,128)S(1)}, f32[1,2,8,2048]{3,0,2,1:T(1,128)S(1)}, u32[]{:S(2)}, u32[]{:S(2)}) collective-permute-start(f32[1,2,8,2048]{3,0,2,1:T(1,128)S(1)} %get-tuple-element.26), channel_id=1, source_target_pairs={{0,2},{1,3},{2,4},{3,5},{4,6},{5,7},{6,0},{7,1},{8,10},{9,11},{10,... | collective-permute-start | bytes 393224 | tf_op jit(solution)/shard_map/ppermute | solution.py:33
  86.7 9.4 %collective-permute-start.4 = (f32[1,2,8,2048]{3,0,2,1:T(1,128)S(1)}, f32[1,2,8,2048]{3,0,2,1:T(1,128)S(1)}, u32[]{:S(2)}, u32[]{:S(2)}) collective-permute-start(f32[1,2,8,2048]{3,0,2,1:T(1,128)S(1)} %get-tuple-element.27), channel_id=1, source_target_pairs={{0,1},{1,2},{2,3},{3,4},{4,5},{5,6},{6,7},{7,0},{8,9},{9,10},{10,1... | collective-permute-start | bytes 393224 | tf_op jit(solution)/shard_map/ppermute | solution.py:33
  86.8 27.3 %collective-permute-start.8 = (f32[1,2,8,2048]{3,0,2,1:T(1,128)S(1)}, f32[1,2,8,2048]{3,0,2,1:T(1,128)S(1)}, u32[]{:S(2)}, u32[]{:S(2)}) collective-permute-start(f32[1,2,8,2048]{3,0,2,1:T(1,128)S(1)} %get-tuple-element.23), channel_id=1, source_target_pairs={{0,5},{1,6},{2,7},{3,0},{4,1},{5,2},{6,3},{7,4},{8,13},{9,14},{10,... | collective-permute-start | bytes 393224 | tf_op jit(solution)/shard_map/ppermute | solution.py:33
  91.5 9.8 %collective-permute-start.6 = (f32[1,2,8,2048]{3,0,2,1:T(1,128)S(1)}, f32[1,2,8,2048]{3,0,2,1:T(1,128)}, u32[]{:S(2)}, u32[]{:S(2)}) collective-permute-start(f32[1,2,8,2048]{3,0,2,1:T(1,128)S(1)} %get-tuple-element.25), channel_id=1, source_target_pairs={{0,3},{1,4},{2,5},{3,6},{4,7},{5,0},{6,1},{7,2},{8,11},{9,12},{10,... | collective-permute-start | bytes 393224 | tf_op jit(solution)/shard_map/ppermute | solution.py:33
  91.5 20.6 %collective-permute-start.7 = (f32[1,2,8,2048]{3,0,2,1:T(1,128)S(1)}, f32[1,2,8,2048]{3,0,2,1:T(1,128)}, u32[]{:S(2)}, u32[]{:S(2)}) collective-permute-start(f32[1,2,8,2048]{3,0,2,1:T(1,128)S(1)} %get-tuple-element.24), channel_id=1, source_target_pairs={{0,4},{1,5},{2,6},{3,7},{4,0},{5,1},{6,2},{7,3},{8,12},{9,13},{10,... | collective-permute-start | bytes 393224 | tf_op jit(solution)/shard_map/ppermute | solution.py:33
  93.5 21.4 %collective-permute-start.9 = (f32[1,2,8,2048]{3,0,2,1:T(1,128)S(1)}, f32[1,2,8,2048]{3,0,2,1:T(1,128)}, u32[]{:S(2)}, u32[]{:S(2)}) collective-permute-start(f32[1,2,8,2048]{3,0,2,1:T(1,128)S(1)} %get-tuple-element.22), channel_id=1, source_target_pairs={{0,6},{1,7},{2,0},{3,1},{4,2},{5,3},{6,4},{7,5},{8,14},{9,15},{10,... | collective-permute-start | bytes 393224 | tf_op jit(solution)/shard_map/ppermute | solution.py:33
  96.8 20.2 %collective-permute-start.10 = (f32[1,2,8,2048]{3,0,2,1:T(1,128)S(1)}, f32[1,2,8,2048]{3,0,2,1:T(1,128)}, u32[]{:S(2)}, u32[]{:S(2)}) collective-permute-start(f32[1,2,8,2048]{3,0,2,1:T(1,128)S(1)} %get-tuple-element.21), channel_id=1, source_target_pairs={{0,7},{1,0},{2,1},{3,2},{4,3},{5,4},{6,5},{7,6},{8,15},{9,8},{10,9... | collective-permute-start | bytes 393224 | tf_op jit(solution)/shard_map/ppermute | solution.py:33
  121.0 4.3 %collective-permute-start.12 = (f32[2,2048]{1,0:T(2,128)S(1)}, f32[2,2048]{1,0:T(2,128)S(1)}, u32[]{:S(2)}, u32[]{:S(2)}) collective-permute-start(f32[2,2048]{1,0:T(2,128)S(1)} %get-tuple-element.40), channel_id=1, source_target_pairs={{0,8},{8,16},{16,24},{24,32},{32,40},{40,48},{48,56},{56,64},{64,7... | collective-permute-start | bytes 49160 | tf_op jit(solution)/shard_map/ppermute | solution.py:46
  122.9 5.1 %collective-permute-start.11 = (f32[2,2048]{1,0:T(2,128)S(1)}, f32[2,2048]{1,0:T(2,128)S(1)}, u32[]{:S(2)}, u32[]{:S(2)}) collective-permute-start(f32[2,2048]{1,0:T(2,128)S(1)} %get-tuple-element.41), channel_id=1, source_target_pairs={{8,0},{16,8},{24,16},{32,24},{40,32},{48,40},{56,48},{64,56},{72,6... | collective-permute-start | bytes 49160 | tf_op jit(solution)/shard_map/ppermute | solution.py:48
  128.1 5.4 %collective-permute-start.13 = (f32[68,2]{1,0:T(8,128)S(1)}, f32[68,2]{1,0:T(8,128)S(1)}, u32[]{:S(2)}, u32[]{:S(2)}) collective-permute-start(f32[68,2]{1,0:T(8,128)S(1)} %get-tuple-element.32), channel_id=1, source_target_pairs={{1,0},{2,1},{3,2},{4,3},{5,4},{6,5},{7,6},{9,8},{10,9},{11,10},{12... | collective-permute-start | bytes 1640 | tf_op jit(solution)/shard_map/ppermute | solution.py:48
  129.4 5.1 %collective-permute-start.14 = (f32[68,2]{1,0:T(8,128)S(1)}, f32[68,2]{1,0:T(8,128)S(1)}, u32[]{:S(2)}, u32[]{:S(2)}) collective-permute-start(f32[68,2]{1,0:T(8,128)S(1)} %get-tuple-element.33), channel_id=1, source_target_pairs={{0,1},{1,2},{2,3},{3,4},{4,5},{5,6},{6,7},{8,9},{9,10},{10,11},{11... | collective-permute-start | bytes 1640 | tf_op jit(solution)/shard_map/ppermute | solution.py:46
  217.6 86.6 %copy-start.1 = (f32[64,2048]{1,0:T(8,128)}, f32[64,2048]{1,0:T(8,128)S(1)}, u32[]{:S(2)}) copy-start(f32[64,2048]{1,0:T(8,128)S(1)} %multiply_subtract_fusion.2) | copy-start | bytes 1572868
  274.9 6.8 %collective-permute-start.16 = (f32[1,2,8,2048]{3,0,2,1:T(1,128)S(1)}, f32[1,2,8,2048]{3,0,2,1:T(1,128)S(1)}, u32[]{:S(2)}, u32[]{:S(2)}) collective-permute-start(f32[1,2,8,2048]{3,0,2,1:T(1,128)S(1)} %get-tuple-element.15), channel_id=1, source_target_pairs={{0,2},{1,3},{2,4},{3,5},{4,6},{5,7},{6,0},{7,1},{8,10},{9,11},{10,... | collective-permute-start | bytes 393224 | tf_op jit(solution)/shard_map/ppermute | solution.py:33
  275.0 9.5 %collective-permute-start.15 = (f32[1,2,8,2048]{3,0,2,1:T(1,128)S(1)}, f32[1,2,8,2048]{3,0,2,1:T(1,128)S(1)}, u32[]{:S(2)}, u32[]{:S(2)}) collective-permute-start(f32[1,2,8,2048]{3,0,2,1:T(1,128)S(1)} %get-tuple-element.16), channel_id=1, source_target_pairs={{0,1},{1,2},{2,3},{3,4},{4,5},{5,6},{6,7},{7,0},{8,9},{9,10},{10,1... | collective-permute-start | bytes 393224 | tf_op jit(solution)/shard_map/ppermute | solution.py:33
  275.9 24.3 %collective-permute-start.19 = (f32[1,2,8,2048]{3,0,2,1:T(1,128)S(1)}, f32[1,2,8,2048]{3,0,2,1:T(1,128)S(1)}, u32[]{:S(2)}, u32[]{:S(2)}) collective-permute-start(f32[1,2,8,2048]{3,0,2,1:T(1,128)S(1)} %get-tuple-element.12), channel_id=1, source_target_pairs={{0,5},{1,6},{2,7},{3,0},{4,1},{5,2},{6,3},{7,4},{8,13},{9,14},{10,... | collective-permute-start | bytes 393224 | tf_op jit(solution)/shard_map/ppermute | solution.py:33
  279.8 9.7 %collective-permute-start.17 = (f32[1,2,8,2048]{3,0,2,1:T(1,128)S(1)}, f32[1,2,8,2048]{3,0,2,1:T(1,128)S(1)}, u32[]{:S(2)}, u32[]{:S(2)}) collective-permute-start(f32[1,2,8,2048]{3,0,2,1:T(1,128)S(1)} %get-tuple-element.14), channel_id=1, source_target_pairs={{0,3},{1,4},{2,5},{3,6},{4,7},{5,0},{6,1},{7,2},{8,11},{9,12},{10,... | collective-permute-start | bytes 393224 | tf_op jit(solution)/shard_map/ppermute | solution.py:33
  279.8 19.8 %collective-permute-start.18 = (f32[1,2,8,2048]{3,0,2,1:T(1,128)S(1)}, f32[1,2,8,2048]{3,0,2,1:T(1,128)S(1)}, u32[]{:S(2)}, u32[]{:S(2)}) collective-permute-start(f32[1,2,8,2048]{3,0,2,1:T(1,128)S(1)} %get-tuple-element.13), channel_id=1, source_target_pairs={{0,4},{1,5},{2,6},{3,7},{4,0},{5,1},{6,2},{7,3},{8,12},{9,13},{10,... | collective-permute-start | bytes 393224 | tf_op jit(solution)/shard_map/ppermute | solution.py:33
  281.8 19.3 %collective-permute-start.20 = (f32[1,2,8,2048]{3,0,2,1:T(1,128)S(1)}, f32[1,2,8,2048]{3,0,2,1:T(1,128)S(1)}, u32[]{:S(2)}, u32[]{:S(2)}) collective-permute-start(f32[1,2,8,2048]{3,0,2,1:T(1,128)S(1)} %get-tuple-element.11), channel_id=1, source_target_pairs={{0,6},{1,7},{2,0},{3,1},{4,2},{5,3},{6,4},{7,5},{8,14},{9,15},{10,... | collective-permute-start | bytes 393224 | tf_op jit(solution)/shard_map/ppermute | solution.py:33
  285.2 17.2 %collective-permute-start.21 = (f32[1,2,8,2048]{3,0,2,1:T(1,128)S(1)}, f32[1,2,8,2048]{3,0,2,1:T(1,128)S(1)}, u32[]{:S(2)}, u32[]{:S(2)}) collective-permute-start(f32[1,2,8,2048]{3,0,2,1:T(1,128)S(1)} %get-tuple-element.10), channel_id=1, source_target_pairs={{0,7},{1,0},{2,1},{3,2},{4,3},{5,4},{6,5},{7,6},{8,15},{9,8},{10,9... | collective-permute-start | bytes 393224 | tf_op jit(solution)/shard_map/ppermute | solution.py:33
  (12 other events, 90.0 us)
